TPU v7x, 128 devices: a whole 4x4x4 slice. The times are simulated.
128 devices in a mesh: space: 32 (over z, y_hi, x), vel: 4 (over y_lo, core).
Axes of the slice: x: 4, y: 4 (y_hi: 2, y_lo: 2; y = y_hi * 2 + y_lo), z: 4, core: 2. Of those that a mesh axis runs over, the one named last changes fastest.
Arguments:
- dist: float32 [128, 10, 32768], P('space', None, 'vel'), may hold values from 0.1 to 2
- phi: float32 [32768], replicated, may hold values from 0.5 to 2
- khat: float32 [32, 1024], replicated, may hold values from 0.2 to 2
- deriv: float32 [3, 10, 10], replicated, may hold values from -2 to 2
- lift: float32 [4, 10, 6], replicated, may hold values from -2.5 to 2.5
- normals: float32 [4, 3], replicated, may hold values from -1 to 1, as said below
- wall_maxw: float32 [32768], P('vel'), may hold values from 0.1 to 1
- free_stream: float32 [32768], P('vel'), may hold values from 0.1 to 1
- inject: float32 [4, 32768], P(None, 'vel'), may hold values from 0 to 1
- nb_local: int32 [128, 4], P('space'), may hold values from 0 to 3
- nb_side: int32 [128, 4], P('space'), may hold values from 0 to 3, as said below
- wall_flag: int32 [128, 4], P('space'), may hold values from 0 to 1
- inj_id: int32 [128, 4], P('space'), may hold values from 0 to 3
Outputs:
- rate: float32 [128, 10, 32768], P('space', None, 'vel')
Inputs may be any that keep to these rules, and one draw needn't show every extreme that they name: nb_side: 0 the neighbour is on the same index of space, 1 on the index below, 2 on the index above, 3 the face lies on the boundary. On every index of space but the first, exactly one face has nb_side 1, and it is face 0 of its element; on every index but the last, exactly one face has nb_side 2, and it is face 1 of its element; no other face has nb_side 1 or 2. Where nb_side is 3, nb_local is 0. Faces are joined in pairs consistently. `normals`: every component has magnitude between 0.4 and 1.
All inputs are finite; a program needn't handle non-finite values.
Results may differ from a plain program's by a relative error of at most 0.0001.
Values sent between devices are 32-bit elements; how exact they have to be, the bound alone decides.
A program may use at most 128 MiB of HBM per device.

v0:
```python
import math

import jax
import jax.numpy as jnp
import numpy as np
import ml_dtypes
from jax import lax
from jax.experimental import pallas as pl
from jax.experimental.pallas import tpu as pltpu
from jax.sharding import PartitionSpec as P

FACES = ((1, 2, 3, 5, 8, 9), (0, 2, 3, 6, 7, 9), (0, 1, 3, 4, 7, 8), (0, 1, 2, 4, 5, 6))
SPEED = 3.0
NODES = 10
ELEMS = 4
GROUP = 4
SLAB = 64
BLOCK = 256
HALF = 136
PACK = 128
TABLE = ELEMS * NODES * 8
HALO = TABLE + 5 * 8
POOL = HALO + 2 * NODES * 8


def split(x):
    hi = x.astype(ml_dtypes.bfloat16)
    lo = (x - hi.astype(np.float64)).astype(ml_dtypes.bfloat16)
    return hi, lo


def tables():
    turn = 2.0 * np.pi
    ka = np.repeat(np.arange(17), 8)
    kl = np.tile(np.arange(8), 17)
    a = np.repeat(np.arange(32), 8)
    bh = np.tile(np.arange(8), 32)
    bl = np.repeat(np.arange(4), 32)
    c = np.tile(np.arange(32), 4)
    angle = turn * ((np.outer(ka, a) % 32) / 32.0 + (np.outer(kl, bh) % 8) / 8.0)
    rows_fwd = np.concatenate([np.cos(angle), -np.sin(angle)], axis=0)
    angle = turn * ((np.outer(bl, bl) % 4) / 4.0 + (np.outer(c, c) % 32) / 32.0)
    co, si = np.cos(angle), np.sin(angle)
    lanes_fwd = np.concatenate(
        [np.concatenate([co, -si], axis=1), np.concatenate([si, co], axis=1)], axis=0
    )
    lanes_bwd = np.concatenate(
        [np.concatenate([co, si], axis=1), np.concatenate([-si, co], axis=1)], axis=0
    )
    angle = turn * ((np.outer(a, ka[:PACK]) % 32) / 32.0 + (np.outer(bh, kl[:PACK]) % 8) / 8.0)
    re, im = 2.0 * np.cos(angle), -2.0 * np.sin(angle)
    sign = np.where(a % 2 == 0, 1.0, -1.0)[:, None]
    angle = turn * ((np.outer(bh, np.arange(8)) % 8) / 8.0)
    re[:, :8] = np.cos(angle) + sign * np.sin(angle)
    im[:, :8] = -np.sin(angle) + sign * np.cos(angle)
    rows_bwd = np.concatenate([re, im], axis=1) * 2.0**-15

    def left(x):
        hi, lo = split(x)
        return np.concatenate([hi, hi, lo], axis=1)

    def right(x):
        hi, lo = split(x)
        return np.concatenate([hi, hi, lo], axis=0)

    angle = turn * np.outer(np.arange(8), bl) / 32.0
    twiddle = np.concatenate([np.cos(angle), np.sin(angle)], axis=0).astype(np.float32)
    lane = np.arange(128)
    mirror = (lane // 32) * 32 + (32 - lane % 32) % 32
    reverse = (lane[:, None] == mirror[None, :]).astype(ml_dtypes.bfloat16)
    return (left(rows_fwd), right(lanes_fwd), right(lanes_bwd), left(rows_bwd), twiddle, reverse)


def halves(x):
    hi = x.astype(jnp.bfloat16)
    lo = (x - hi.astype(jnp.float32)).astype(jnp.bfloat16)
    return hi, lo


def dot_left(table, x):
    hi, lo = halves(x)
    return jnp.dot(
        table, jnp.concatenate([hi, lo, hi], axis=0), preferred_element_type=jnp.float32
    )


def dot_right(x, table):
    hi, lo = halves(x)
    return jnp.dot(
        jnp.concatenate([hi, lo, hi], axis=1), table, preferred_element_type=jnp.float32
    )


def by_rows(x, y):
    return jnp.concatenate([x, y], axis=0)


def by_lanes(x, y):
    return jnp.concatenate([x, y], axis=1)


def turned(re, im, cos, sin):
    count = re.shape[0] // 8
    re = re.reshape(count, 8, 128)
    im = im.reshape(count, 8, 128)
    out_re = re * cos[None] - im * sin[None]
    out_im = re * sin[None] + im * cos[None]
    return out_re.reshape(count * 8, 128), out_im.reshape(count * 8, 128)


def collide(x, phi, sym, rows_fwd, lanes_fwd, lanes_bwd, rows_bwd, cos, sin):
    y = dot_left(rows_fwd, by_lanes(x * phi, x))
    wr, wi = turned(y[:HALF, :128], y[HALF:, :128], cos, -sin)
    fr, fi = turned(y[:HALF, 128:], y[HALF:, 128:], cos, -sin)
    s = dot_right(by_rows(by_lanes(wr, wi), by_lanes(fr, fi)), lanes_fwd)
    wr, wi, fr, fi = s[:HALF, :128], s[:HALF, 128:], s[HALF:, :128], s[HALF:, 128:]
    wr, wi = wr * 2.0**-15, wi * 2.0**-15

    def packed(re, im):
        first = re[:8] - im[PACK:]
        second = im[:8] + re[PACK:]
        return by_lanes(by_rows(first, re[8:PACK]), by_rows(second, im[8:PACK]))

    gain = packed(wr * fr - wi * fi, wr * fi + wi * fr)
    loss = packed(sym * fr, sym * fi)
    b = dot_right(by_rows(gain, loss), lanes_bwd)
    gr, gi = turned(b[:PACK, :128], b[:PACK, 128:], cos, sin)
    lr, li = turned(b[PACK:, :128], b[PACK:, 128:], cos, sin)
    z = dot_left(rows_bwd, by_rows(by_lanes(gr, lr), by_lanes(gi, li)))
    return z[:, :128] - x * z[:, 128:]


def kernel(
    space,
    dist,
    phi,
    khat,
    deriv,
    lift,
    normals,
    wall,
    free,
    inject,
    nb_local,
    nb_side,
    wall_flag,
    inj_id,
    rows_fwd,
    lanes_fwd,
    lanes_bwd,
    rows_bwd,
    twiddle,
    reverse,
    out,
    pool,
    block,
    result,
    back,
    moved,
    diff,
    negwall,
    straight,
    mirrored,
    sym,
    wallsum,
    halo_out,
    halo_in,
    sums_out,
    sums_in,
    fwd_send,
    fwd_recv,
    bwd_send,
    bwd_recv,
    halo_send,
    halo_recv,
    sums_send,
    sums_recv,
):
    f32 = jnp.float32
    me = lax.axis_index("vel")
    here = lax.axis_index("space")
    above = lax.rem(here + 1, space)
    below = lax.rem(here + space - 1, space)
    core = lax.rem(me, 2)
    flip = 1 - 2 * core
    across = lax.rem(me + 2, GROUP)
    partners = (across, across + flip, me + flip)

    def rows(start, count=8):
        return pl.ds(pl.multiple_of(start, 8), count)

    def forward(n, q):
        to = partners[q]
        return pltpu.make_async_remote_copy(
            src_ref=pool.at[pl.ds((to * NODES + n) * 8, 8)],
            dst_ref=block.at[pl.ds(n * 32 + me * 8, 8)],
            send_sem=fwd_send.at[n, q],
            recv_sem=fwd_recv.at[n, q],
            device_id={"vel": to},
        )

    def backward(n, q):
        to = partners[q]
        return pltpu.make_async_remote_copy(
            src_ref=result.at[rows(n * BLOCK + to * SLAB, SLAB)],
            dst_ref=back.at[rows((me * NODES + n) * SLAB, SLAB)],
            send_sem=bwd_send.at[n, q],
            recv_sem=bwd_recv.at[n, q],
            device_id={"vel": to},
        )

    def halo(side):
        return pltpu.make_async_remote_copy(
            src_ref=halo_out.at[side],
            dst_ref=halo_in.at[side],
            send_sem=halo_send.at[side],
            recv_sem=halo_recv.at[side],
            device_id={"space": below if side else above},
        )

    def sums(q):
        return pltpu.make_async_remote_copy(
            src_ref=sums_out,
            dst_ref=sums_in.at[q],
            send_sem=sums_send.at[q],
            recv_sem=sums_recv.at[q],
            device_id={"vel": partners[q]},
        )

    barrier = pltpu.get_barrier_semaphore()
    for to in partners:
        pl.semaphore_signal(barrier, inc=1, device_id={"vel": to})
    for to in (above, below):
        pl.semaphore_signal(barrier, inc=1, device_id={"space": to})
    pl.semaphore_wait(barrier, 5)

    @pl.loop(0, NODES)
    def _(n):
        for e in range(ELEMS):
            for a in range(8):
                pool[(e * NODES + n) * 8 + a] = dist[
                    pl.ds(n * BLOCK + a * 32 + e, 8, stride=4), :
                ]
        for q in range(3):
            forward(n, q).start()
        for a in range(8):
            block[n * 32 + me * 8 + a] = pool[(me * NODES + n) * 8 + a]

    up_elem = jnp.int32(0)
    down_elem = jnp.int32(0)
    for e in range(ELEMS):
        up_elem = up_elem + jnp.where(nb_side[e, 1] == 2, e, 0)
        down_elem = down_elem + jnp.where(nb_side[e, 0] == 1, e, 0)
    for side, elem, face in ((0, up_elem, 1), (1, down_elem, 0)):
        for k in range(6):
            for a in range(8):
                halo_out[side, k * 8 + a] = pool[(elem * NODES + FACES[face][k]) * 8 + a]
        halo(side).start()

    for q in range(4):
        for a in range(8):
            pool[TABLE + q * 8 + a] = inject[pl.ds(a * 32 + q, 8, stride=4), :]
    for a in range(8):
        pool[TABLE + 32 + a] = free[a * 8 : a * 8 + 8, :]

    sub = lax.broadcasted_iota(jnp.int32, (8, 128), 0)
    lane = lax.broadcasted_iota(jnp.int32, (8, 128), 1)

    def grid(i):
        return SPEED * ((2.0 * i.astype(f32) + 1.0) / 32.0 - 1.0)

    v2 = grid(lane % 32)
    v1 = grid(sub * 4 + lane // 32)

    def normal_speed(j, v0, v1):
        return normals[j, 0] * v0 + normals[j, 1] * v1 + normals[j, 2] * v2

    def partial_sums(i, carry):
        a = i // 4
        v0 = grid(me * 8 + a)
        b = (lax.rem(i, 4) * 2 + sub // 4) * 4 + lane // 32
        got = [dist[rows(n * BLOCK + i * 8), :] for n in range(NODES)]
        new = []
        for j in range(4):
            pos = jnp.maximum(normal_speed(j, v0, grid(b)), 0.0)
            for k in range(6):
                new.append(carry[j * 6 + k] + pos * got[FACES[j][k]])
        return tuple(new)

    zero = jnp.zeros((8, 128), f32)
    nums = lax.fori_loop(0, 32, partial_sums, (zero,) * 24)

    def partial_dens(a, carry):
        v0 = grid(me * 8 + a)
        new = []
        for j in range(4):
            value = jnp.minimum(normal_speed(j, v0, v1), 0.0) * wall[rows(a * 8), :]
            negwall[rows((j * 8 + a) * 8), :] = value
            new.append(carry[j] - value)
        return tuple(new)

    dens = lax.fori_loop(0, 8, partial_dens, (zero,) * 4)
    mine = zero
    for i, x in enumerate(nums):
        x = x + pltpu.roll(x, 4, 0)
        mine = jnp.where(lane == i, jnp.sum(x, axis=1, keepdims=True), mine)
    for j, x in enumerate(dens):
        x = jnp.broadcast_to(jnp.sum(x, axis=0, keepdims=True), (8, 128))
        mine = jnp.where(lane == 24 + j, jnp.sum(x, axis=1, keepdims=True), mine)
    sums_out[...] = mine
    for q in range(3):
        sums(q).start()

    for i in range(8):
        x = khat[:, i * 128 : (i + 1) * 128]
        straight[i * 32 : (i + 1) * 32, :] = x
    x = straight[...]
    x0 = x.astype(jnp.bfloat16)
    x = x - x0.astype(f32)
    x1 = x.astype(jnp.bfloat16)
    x2 = (x - x1.astype(f32)).astype(jnp.bfloat16)
    rev = reverse[...]
    mirrored[...] = (
        jnp.dot(x0, rev, preferred_element_type=f32) + jnp.dot(x1, rev, preferred_element_type=f32)
    ) + jnp.dot(x2, rev, preferred_element_type=f32)
    group = lax.broadcasted_iota(jnp.int32, (32, 128), 1) // 32

    def regroup(source, place):
        total = jnp.zeros((32, 128), f32)
        for kh in range(4):
            kb = place(kh)
            tile, offset = kb // 4, kb % 4
            x = source[tile * 32 : (tile + 1) * 32, :]
            shift = (kh - offset) % 4 * 32
            if shift:
                x = pltpu.roll(x, shift, 1)
            total = jnp.where(group == kh, x, total)
        return total

    for kl in range(8):
        even = regroup(straight, lambda kh: kl + 8 * kh)
        odd = regroup(mirrored, lambda kh: (32 - kl - 8 * kh) % 32)
        moved[pl.ds(kl, 32, stride=8), :] = even
        moved[pl.ds(BLOCK + kl, 32, stride=8), :] = odd
    for ka in range(17):
        other = BLOCK + (32 - ka) % 32 * 8
        sym[ka * 8 : ka * 8 + 8, :] = 0.5 * (
            moved[ka * 8 : ka * 8 + 8, :] + moved[other : other + 8, :]
        )

    for side, face in ((0, 1), (1, 0)):
        halo(side).wait_recv()
        for k in range(6):
            start = HALO + (side * NODES + FACES[face][k]) * 8
            for a in range(8):
                pool[start + a] = halo_in[side, k * 8 + a]

    @pl.loop(0, 8)
    def _(a):
        v0 = grid(me * 8 + a)
        negs = [jnp.minimum(normal_speed(j, v0, v1), 0.0) for j in range(4)]

        @pl.loop(0, ELEMS)
        def _(e):
            for j in range(4):
                side = nb_side[e, j]
                inner = jnp.where(side == 3, 0, 8)
                edge = TABLE + jnp.where(wall_flag[e, j] == 1, inj_id[e, j], 4) * 8
                near = nb_local[e, j] * (NODES * 8)
                far = HALO + jnp.where(side == 2, NODES * 8, 0)
                base = jnp.where(side == 3, edge, jnp.where(side == 0, near, far)) + a
                for k in range(6):
                    outer = pool[base + inner * FACES[j ^ 1][k]]
                    trace = pool[(e * NODES + FACES[j][k]) * 8 + a]
                    diff[j * 6 + k, rows(e * 8), :] = negs[j] * (trace - outer)

        @pl.loop(0, NODES // 2)
        def _(pair):
            acc = [[zero] * ELEMS for _ in range(2)]
            for m in range(NODES):
                for i in range(2):
                    n = pair * 2 + i
                    c = deriv[n, 0, m] * v0 + deriv[n, 1, m] * v1 + deriv[n, 2, m] * v2
                    for e in range(ELEMS):
                        f = pool[(e * NODES + m) * 8 + a]
                        acc[i][e] = acc[i][e] - c * f
            for j in range(4):
                for k in range(6):
                    for i in range(2):
                        c = lift[k, j, pair * 2 + i]
                        for e in range(ELEMS):
                            d = diff[j * 6 + k, e * 8 : e * 8 + 8, :]
                            acc[i][e] = acc[i][e] + c * d
            for i in range(2):
                for e in range(ELEMS):
                    moved[rows((e * NODES + pair * 2 + i) * SLAB + a * 8), :] = acc[i][e]

    cos = twiddle[0:8, :]
    sin = twiddle[8:16, :]

    @pl.loop(0, NODES)
    def _(n):
        for q in range(3):
            forward_in(n, q, block, pool, fwd_send, fwd_recv, partners, rows).wait_recv()
        result[rows(n * BLOCK, BLOCK), :] = collide(
            block[pl.ds(n * 32, 32)].reshape(BLOCK, 128),
            phi[...],
            sym[...],
            rows_fwd[...],
            lanes_fwd[...],
            lanes_bwd[...],
            rows_bwd[...],
            cos,
            sin,
        )
        for q in range(3):
            backward(n, q).start()

    total = sums_out[...]
    for q in range(3):
        sums(q).wait_recv()
    for q in range(3):
        total = total + sums_in[q]
    for j in range(4):
        mask = zero
        for e in range(ELEMS):
            on = jnp.where(nb_side[e, j] == 3, jnp.where(wall_flag[e, j] == 1, 1.0, 0.0), 0.0)
            mask = jnp.where(sub % 4 == e, on, mask)
        den = jnp.broadcast_to(total[:, 24 + j : 25 + j], (8, 128))
        sigma = [
            jnp.broadcast_to(total[:, j * 6 + k : j * 6 + k + 1], (8, 128)) / den * mask
            for k in range(6)
        ]
        for n in range(NODES):
            part = lift[0, j, n] * sigma[0]
            for k in range(1, 6):
                part = part + lift[k, j, n] * sigma[k]
            wallsum[(j * NODES + n) * 8 : (j * NODES + n) * 8 + 8, :] = part

    @pl.loop(0, ELEMS)
    def _(e):
        @pl.loop(0, NODES)
        def _(n):
            parts = [
                jnp.broadcast_to(wallsum[pl.ds((j * NODES + n) * 8 + e, 1), :], (8, 128))
                for j in range(4)
            ]
            for a in range(8):
                x = moved[rows((e * NODES + n) * SLAB + a * 8), :]
                for j in range(4):
                    x = x - parts[j] * negwall[(j * 8 + a) * 8 : (j * 8 + a) * 8 + 8, :]
                moved[rows((e * NODES + n) * SLAB + a * 8), :] = x

    @pl.loop(0, NODES)
    def _(n):
        for a in range(8):
            out[pl.ds(n * BLOCK + a * 32 + me, 8, stride=4), :] = (
                result[rows(n * BLOCK + me * SLAB + a * 8), :]
                + moved[rows((me * NODES + n) * SLAB + a * 8), :]
            )
        for q in range(3):
            backward_in(n, q, back, result, bwd_send, bwd_recv, partners, rows).wait_recv()
            e = partners[q]
            for a in range(8):
                at = rows((e * NODES + n) * SLAB + a * 8)
                out[pl.ds(n * BLOCK + a * 32 + e, 8, stride=4), :] = back[at, :] + moved[at, :]

    @pl.loop(0, NODES)
    def _(n):
        for q in range(3):
            forward(n, q).wait_send()
            backward(n, q).wait_send()

    for side in range(2):
        halo(side).wait_send()
    for q in range(3):
        sums(q).wait_send()


def forward_in(n, q, block, pool, send, recv, partners, rows):
    return pltpu.make_async_remote_copy(
        src_ref=pool.at[pl.ds(0, 8)],
        dst_ref=block.at[pl.ds(n * 32 + partners[q] * 8, 8)],
        send_sem=send.at[n, q],
        recv_sem=recv.at[n, q],
        device_id={"vel": partners[q]},
    )


def backward_in(n, q, back, result, send, recv, partners, rows):
    return pltpu.make_async_remote_copy(
        src_ref=result.at[rows(0, SLAB)],
        dst_ref=back.at[rows((partners[q] * NODES + n) * SLAB, SLAB)],
        send_sem=send.at[n, q],
        recv_sem=recv.at[n, q],
        device_id={"vel": partners[q]},
    )


def solution(mesh):
    space = mesh.shape["space"]
    constants = tables()

    def local(
        dist,
        phi,
        khat,
        deriv,
        lift,
        normals,
        wall_maxw,
        free_stream,
        inject,
        nb_local,
        nb_side,
        wall_flag,
        inj_id,
    ):
        lines = dist.transpose(1, 0, 2).reshape(NODES, ELEMS, SLAB, 128)
        lines = lines.transpose(0, 2, 1, 3).reshape(NODES * BLOCK, 128)
        profiles = inject.reshape(4, SLAB, 128).transpose(1, 0, 2).reshape(BLOCK, 128)
        vmem = pl.BlockSpec(memory_space=pltpu.VMEM)
        smem = pl.BlockSpec(memory_space=pltpu.SMEM)
        f32 = jnp.float32
        dma = pltpu.SemaphoreType.DMA

        def body(*refs):
            kernel(space, *refs)

        rate = pl.pallas_call(
            body,
            out_shape=jax.ShapeDtypeStruct((NODES * BLOCK, 128), f32),
            in_specs=[vmem] * 3 + [smem] * 3 + [vmem] * 3 + [smem] * 4 + [vmem] * 6,
            out_specs=vmem,
            scratch_shapes=[
                pltpu.VMEM((POOL, 8, 128), f32),
                pltpu.VMEM((NODES * 32, 8, 128), f32),
                pltpu.VMEM((NODES * BLOCK, 128), f32),
                pltpu.VMEM((ELEMS * NODES * SLAB, 128), f32),
                pltpu.VMEM((ELEMS * NODES * SLAB, 128), f32),
                pltpu.VMEM((24, ELEMS * 8, 128), f32),
                pltpu.VMEM((4 * SLAB, 128), f32),
                pltpu.VMEM((BLOCK, 128), f32),
                pltpu.VMEM((BLOCK, 128), f32),
                pltpu.VMEM((HALF, 128), f32),
                pltpu.VMEM((4 * NODES * 8, 128), f32),
                pltpu.VMEM((2, 6 * 8, 8, 128), f32),
                pltpu.VMEM((2, 6 * 8, 8, 128), f32),
                pltpu.VMEM((8, 128), f32),
                pltpu.VMEM((3, 8, 128), f32),
                dma((NODES, 3)),
                dma((NODES, 3)),
                dma((NODES, 3)),
                dma((NODES, 3)),
                dma((2,)),
                dma((2,)),
                dma((3,)),
                dma((3,)),
            ],
            compiler_params=pltpu.CompilerParams(
                collective_id=0, has_side_effects=True, vmem_limit_bytes=40 * 2**20
            ),
            name="rate",
        )(
            lines,
            phi.reshape(BLOCK, 128),
            khat,
            deriv.transpose(1, 0, 2),
            lift.transpose(2, 0, 1),
            normals,
            wall_maxw.reshape(SLAB, 128),
            free_stream.reshape(SLAB, 128),
            profiles,
            nb_local,
            nb_side,
            wall_flag,
            inj_id,
            *[jnp.asarray(c) for c in constants],
        )
        rate = rate.reshape(NODES, SLAB, ELEMS, 128).transpose(0, 2, 1, 3)
        return rate.reshape(NODES, ELEMS, SLAB * 128).transpose(1, 0, 2)

    return jax.shard_map(
        local,
        mesh=mesh,
        in_specs=(
            P("space", None, "vel"),
            P(),
            P(),
            P(),
            P(),
            P(),
            P("vel"),
            P("vel"),
            P(None, "vel"),
            P("space", None),
            P("space", None),
            P("space", None),
            P("space", None),
        ),
        out_specs=P("space", None, "vel"),
        check_vma=False,
    )
```

profile of v0, /device:TPU:1, one launch (start us, length us, event | category | flops | bytes accessed | tf_op | source)
XLA Modules:
  0.0 59.7 jit_solution(241949984397409328)
XLA Ops:
  0.0 0.0 copy-start
  0.0 1.3 %copy-done = f32[4,10,8192]{2,0,1:T(4,128)S(1)} copy-done((f32[4,10,8192]{2,0,1:T(4,128)S(1)}, f32[4,10,8192]{2,0,1:T(4,128)}, u32[]{:S(2)}) %copy-start) | copy-done | bytes 1310744
  1.3 0.0 copy-start.1
  1.3 1.0 %copy-done.1 = bf16[272,768]{1,0:T(8,128)(2,1)S(1)} copy-done((bf16[272,768]{1,0:T(8,128)(2,1)S(1)}, bf16[272,768]{1,0:T(8,128)(2,1)}, u32[]{:S(2)}) %copy-start.1) | copy-done | bytes 417816
  2.3 0.0 copy-start.2
  2.3 1.0 %copy-done.2 = bf16[256,768]{1,0:T(8,128)(2,1)S(1)} copy-done((bf16[256,768]{1,0:T(8,128)(2,1)S(1)}, bf16[256,768]{1,0:T(8,128)(2,1)}, u32[]{:S(2)}) %copy-start.2) | copy-done | bytes 393240
  3.3 0.0 copy-start.3
  3.3 1.0 %copy-done.3 = bf16[768,256]{1,0:T(8,128)(2,1)S(1)} copy-done((bf16[768,256]{1,0:T(8,128)(2,1)S(1)}, bf16[768,256]{1,0:T(8,128)(2,1)}, u32[]{:S(2)}) %copy-start.3) | copy-done | bytes 393240
  4.3 0.0 copy-start.4
  4.3 1.0 %copy-done.4 = bf16[768,256]{1,0:T(8,128)(2,1)S(1)} copy-done((bf16[768,256]{1,0:T(8,128)(2,1)S(1)}, bf16[768,256]{1,0:T(8,128)(2,1)}, u32[]{:S(2)}) %copy-start.4) | copy-done | bytes 393240
  5.3 0.0 copy-start.5
  5.3 0.9 %copy-done.5 = f32[32768]{0:T(1024)S(1)} copy-done((f32[32768]{0:T(1024)S(1)}, f32[32768]{0:T(1024)}, u32[]{:S(2)}) %copy-start.5) | copy-done | bytes 131096
  6.2 0.0 copy-start.6
  6.2 0.9 %copy-done.6 = f32[32,1024]{1,0:T(8,128)S(1)} copy-done((f32[32,1024]{1,0:T(8,128)S(1)}, f32[32,1024]{1,0:T(8,128)}, u32[]{:S(2)}) %copy-start.6) | copy-done | bytes 131096
  7.1 0.0 copy-start.7
  7.1 0.9 %copy-done.7 = f32[4,8192]{1,0:T(4,128)S(1)} copy-done((f32[4,8192]{1,0:T(4,128)S(1)}, f32[4,8192]{1,0:T(4,128)}, u32[]{:S(2)}) %copy-start.7) | copy-done | bytes 131096
  8.0 0.0 copy-start.8
  8.0 0.8 %copy-done.8 = f32[8192]{0:T(1024)S(1)} copy-done((f32[8192]{0:T(1024)S(1)}, f32[8192]{0:T(1024)}, u32[]{:S(2)}) %copy-start.8) | copy-done | bytes 32792
  8.8 0.0 copy-start.9
  8.8 0.8 %copy-done.9 = f32[8192]{0:T(1024)S(1)} copy-done((f32[8192]{0:T(1024)S(1)}, f32[8192]{0:T(1024)}, u32[]{:S(2)}) %copy-start.9) | copy-done | bytes 32792
  9.5 0.0 copy-start.10
  9.5 0.8 %copy-done.10 = bf16[128,128]{1,0:T(8,128)(2,1)S(1)} copy-done((bf16[128,128]{1,0:T(8,128)(2,1)S(1)}, bf16[128,128]{1,0:T(8,128)(2,1)}, u32[]{:S(2)}) %copy-start.10) | copy-done | bytes 32792
  10.3 0.0 copy-start.11
  10.3 0.7 %copy-done.11 = f32[3,10,10]{2,0,1:T(4,128)S(1)} copy-done((f32[3,10,10]{2,0,1:T(4,128)S(1)}, f32[3,10,10]{2,0,1:T(4,128)}, u32[]{:S(2)}) %copy-start.11) | copy-done | bytes 1224
  11.0 0.0 copy-start.12
  11.0 0.7 %copy-done.12 = f32[4,10,6]{1,0,2:T(4,128)S(1)} copy-done((f32[4,10,6]{1,0,2:T(4,128)S(1)}, f32[4,10,6]{1,0,2:T(4,128)}, u32[]{:S(2)}) %copy-start.12) | copy-done | bytes 984
  11.7 0.0 copy-start.13
  11.7 0.7 %copy-done.13 = f32[16,128]{1,0:T(8,128)S(1)} copy-done((f32[16,128]{1,0:T(8,128)S(1)}, f32[16,128]{1,0:T(8,128)}, u32[]{:S(2)}) %copy-start.13) | copy-done | bytes 8216
  12.4 0.0 copy-start.14
  12.4 0.7 %copy-done.14 = f32[4,3]{1,0:T(4,128)S(1)} copy-done((f32[4,3]{1,0:T(4,128)S(1)}, f32[4,3]{1,0:T(4,128)}, u32[]{:S(2)}) %copy-start.14) | copy-done | bytes 72
  13.1 0.0 copy-start.15
  13.1 0.7 %copy-done.15 = s32[4,4]{1,0:T(4,128)S(1)} copy-done((s32[4,4]{1,0:T(4,128)S(1)}, s32[4,4]{1,0:T(4,128)}, u32[]{:S(2)}) %copy-start.15) | copy-done | bytes 88
  13.8 0.0 copy-start.16
  13.8 0.7 %copy-done.16 = s32[4,4]{1,0:T(4,128)S(1)} copy-done((s32[4,4]{1,0:T(4,128)S(1)}, s32[4,4]{1,0:T(4,128)}, u32[]{:S(2)}) %copy-start.16) | copy-done | bytes 88
  14.5 0.0 copy-start.17
  14.5 0.7 %copy-done.17 = s32[4,4]{1,0:T(4,128)S(1)} copy-done((s32[4,4]{1,0:T(4,128)S(1)}, s32[4,4]{1,0:T(4,128)}, u32[]{:S(2)}) %copy-start.17) | copy-done | bytes 88
  15.2 0.0 copy-start.18
  15.2 0.7 %copy-done.18 = s32[4,4]{1,0:T(4,128)S(1)} copy-done((s32[4,4]{1,0:T(4,128)S(1)}, s32[4,4]{1,0:T(4,128)}, u32[]{:S(2)}) %copy-start.18) | copy-done | bytes 88
  15.8 42.7 %rate.1 = f32[2560,128]{1,0:T(8,128)S(1)} custom-call(f32[2560,128]{1,0:T(8,128)S(1)} %bitcast.25, f32[256,128]{1,0:T(8,128)S(1)} %bitcast.26, f32[32,1024]{1,0:T(8,128)S(1)} %copy-done.6, f32[10,3,10]{2,1,0:T(4,128)S(1)} %bitcast.30, f32[6,4,10]{2,1,0:T(4,128)S(1)} %bitcast.31, f32[4,3]{1,0:T(4,128)S(1)} %copy-done.14, f32[64,128]{1,0:T(8,128)S(1)} %bitcast.28, ...), custom_call_target="tpu_custom_call" | custom-call | tf_op jit(solution)/shard_map/rate/pallas_call | solution.py:530
  58.6 1.1 %copy.23 = f32[4,10,8192]{2,0,1:T(4,128)} copy(f32[4,10,8192]{2,0,1:T(4,128)S(1)} %bitcast.24) | data formatting | bytes 2621440
Async XLA Ops:
  0.0 1.3 %copy-start = (f32[4,10,8192]{2,0,1:T(4,128)S(1)}, f32[4,10,8192]{2,0,1:T(4,128)}, u32[]{:S(2)}) copy-start(f32[4,10,8192]{2,0,1:T(4,128)} %param.19) | copy-start | bytes 3932164
  1.3 1.0 %copy-start.1 = (bf16[272,768]{1,0:T(8,128)(2,1)S(1)}, bf16[272,768]{1,0:T(8,128)(2,1)}, u32[]{:S(2)}) copy-start(bf16[272,768]{1,0:T(8,128)(2,1)} %constant.12.clone.refs_13_) | copy-start | bytes 1253380
  2.3 1.0 %copy-start.2 = (bf16[256,768]{1,0:T(8,128)(2,1)S(1)}, bf16[256,768]{1,0:T(8,128)(2,1)}, u32[]{:S(2)}) copy-start(bf16[256,768]{1,0:T(8,128)(2,1)} %constant.15.clone.refs_16_) | copy-start | bytes 1179652
  3.3 1.0 %copy-start.3 = (bf16[768,256]{1,0:T(8,128)(2,1)S(1)}, bf16[768,256]{1,0:T(8,128)(2,1)}, u32[]{:S(2)}) copy-start(bf16[768,256]{1,0:T(8,128)(2,1)} %constant.14.clone.refs_15_) | copy-start | bytes 1179652
  4.3 1.0 %copy-start.4 = (bf16[768,256]{1,0:T(8,128)(2,1)S(1)}, bf16[768,256]{1,0:T(8,128)(2,1)}, u32[]{:S(2)}) copy-start(bf16[768,256]{1,0:T(8,128)(2,1)} %constant.13.clone.refs_14_) | copy-start | bytes 1179652
  5.3 0.9 %copy-start.5 = (f32[32768]{0:T(1024)S(1)}, f32[32768]{0:T(1024)}, u32[]{:S(2)}) copy-start(f32[32768]{0:T(1024)} %param.20) | copy-start | bytes 393220
  6.2 0.9 %copy-start.6 = (f32[32,1024]{1,0:T(8,128)S(1)}, f32[32,1024]{1,0:T(8,128)}, u32[]{:S(2)}) copy-start(f32[32,1024]{1,0:T(8,128)} %refs_2_.1) | copy-start | bytes 393220
  7.1 0.9 %copy-start.7 = (f32[4,8192]{1,0:T(4,128)S(1)}, f32[4,8192]{1,0:T(4,128)}, u32[]{:S(2)}) copy-start(f32[4,8192]{1,0:T(4,128)} %param.27) | copy-start | bytes 393220
  8.0 0.8 %copy-start.8 = (f32[8192]{0:T(1024)S(1)}, f32[8192]{0:T(1024)}, u32[]{:S(2)}) copy-start(f32[8192]{0:T(1024)} %param.25) | copy-start | bytes 98308
  8.8 0.8 %copy-start.9 = (f32[8192]{0:T(1024)S(1)}, f32[8192]{0:T(1024)}, u32[]{:S(2)}) copy-start(f32[8192]{0:T(1024)} %param.26) | copy-start | bytes 98308
  9.5 0.8 %copy-start.10 = (bf16[128,128]{1,0:T(8,128)(2,1)S(1)}, bf16[128,128]{1,0:T(8,128)(2,1)}, u32[]{:S(2)}) copy-start(bf16[128,128]{1,0:T(8,128)(2,1)} %constant.17.clone.refs_18_) | copy-start | bytes 98308
  10.3 0.7 %copy-start.11 = (f32[3,10,10]{2,0,1:T(4,128)S(1)}, f32[3,10,10]{2,0,1:T(4,128)}, u32[]{:S(2)}) copy-start(f32[3,10,10]{2,0,1:T(4,128)} %param.22) | copy-start | bytes 3604
  11.0 0.7 %copy-start.12 = (f32[4,10,6]{1,0,2:T(4,128)S(1)}, f32[4,10,6]{1,0,2:T(4,128)}, u32[]{:S(2)}) copy-start(f32[4,10,6]{1,0,2:T(4,128)} %param.23) | copy-start | bytes 2884
  11.7 0.7 %copy-start.13 = (f32[16,128]{1,0:T(8,128)S(1)}, f32[16,128]{1,0:T(8,128)}, u32[]{:S(2)}) copy-start(f32[16,128]{1,0:T(8,128)} %constant.16.clone.refs_17_) | copy-start | bytes 24580
  12.4 0.7 %copy-start.14 = (f32[4,3]{1,0:T(4,128)S(1)}, f32[4,3]{1,0:T(4,128)}, u32[]{:S(2)}) copy-start(f32[4,3]{1,0:T(4,128)} %refs_5_.1) | copy-start | bytes 148
  13.1 0.7 %copy-start.15 = (s32[4,4]{1,0:T(4,128)S(1)}, s32[4,4]{1,0:T(4,128)}, u32[]{:S(2)}) copy-start(s32[4,4]{1,0:T(4,128)} %refs_9_.1) | copy-start | bytes 196
  13.8 0.7 %copy-start.16 = (s32[4,4]{1,0:T(4,128)S(1)}, s32[4,4]{1,0:T(4,128)}, u32[]{:S(2)}) copy-start(s32[4,4]{1,0:T(4,128)} %refs_10_.1) | copy-start | bytes 196
  14.5 0.7 %copy-start.17 = (s32[4,4]{1,0:T(4,128)S(1)}, s32[4,4]{1,0:T(4,128)}, u32[]{:S(2)}) copy-start(s32[4,4]{1,0:T(4,128)} %refs_11_.1) | copy-start | bytes 196
  15.2 0.7 %copy-start.18 = (s32[4,4]{1,0:T(4,128)S(1)}, s32[4,4]{1,0:T(4,128)}, u32[]{:S(2)}) copy-start(s32[4,4]{1,0:T(4,128)} %refs_12_.1) | copy-start | bytes 196
where the time goes:
time: 60.5 us; the launch traced here: 59.7 us
  Pallas kernels  42.7 us (71%)
  local copies, waits for them, and re-layouts  16.9 us (28%)
    pallas_call x1, Pallas kernels, local(): pl.pallas_call(body, out_shape=jax.ShapeDtypeStruct((NODES * BLOCK, 128),...  42.7 us
    unnamed x39, local copies, waits for them, and re-layouts  16.9 us

commit v1 on v0

--- a/solution.py
+++ b/solution.py
@@ -132,26 +132,45 @@
 
 def kernel(
     space,
+    dist_in,
+    phi_in,
+    khat_in,
+    wall_in,
+    free_in,
+    inject_in,
+    rows_fwd_in,
+    lanes_fwd_in,
+    lanes_bwd_in,
+    rows_bwd_in,
+    twiddle_in,
+    reverse_in,
+    deriv_in,
+    lift_in,
+    normals_in,
+    nb_local_in,
+    nb_side_in,
+    wall_flag_in,
+    inj_id_in,
+    out,
     dist,
     phi,
     khat,
-    deriv,
-    lift,
-    normals,
     wall,
     free,
     inject,
-    nb_local,
-    nb_side,
-    wall_flag,
-    inj_id,
     rows_fwd,
     lanes_fwd,
     lanes_bwd,
     rows_bwd,
     twiddle,
     reverse,
-    out,
+    deriv,
+    lift,
+    normals,
+    nb_local,
+    nb_side,
+    wall_flag,
+    inj_id,
     pool,
     block,
     result,
@@ -167,6 +186,8 @@
     halo_in,
     sums_out,
     sums_in,
+    dist_sem,
+    load_sem,
     fwd_send,
     fwd_recv,
     bwd_send,
@@ -227,15 +248,49 @@
             device_id={"vel": partners[q]},
         )
 
+    def dist_load(n):
+        part = rows(n * BLOCK, BLOCK)
+        return pltpu.make_async_copy(dist_in.at[part], dist.at[part], dist_sem.at[n])
+
+    pairs = (
+        (nb_side_in, nb_side),
+        (inject_in, inject),
+        (free_in, free),
+        (normals_in, normals),
+        (wall_in, wall),
+        (khat_in, khat),
+        (reverse_in, reverse),
+        (nb_local_in, nb_local),
+        (wall_flag_in, wall_flag),
+        (inj_id_in, inj_id),
+        (deriv_in, deriv),
+        (lift_in, lift),
+        (phi_in, phi),
+        (rows_fwd_in, rows_fwd),
+        (lanes_fwd_in, lanes_fwd),
+        (twiddle_in, twiddle),
+        (lanes_bwd_in, lanes_bwd),
+        (rows_bwd_in, rows_bwd),
+    )
+    loads = [
+        pltpu.make_async_copy(source, target, load_sem.at[i])
+        for i, (source, target) in enumerate(pairs)
+    ]
+
     barrier = pltpu.get_barrier_semaphore()
     for to in partners:
         pl.semaphore_signal(barrier, inc=1, device_id={"vel": to})
     for to in (above, below):
         pl.semaphore_signal(barrier, inc=1, device_id={"space": to})
+    for n in range(NODES):
+        dist_load(n).start()
+    for load in loads:
+        load.start()
     pl.semaphore_wait(barrier, 5)
 
     @pl.loop(0, NODES)
     def _(n):
+        dist_load(n).wait()
         for e in range(ELEMS):
             for a in range(8):
                 pool[(e * NODES + n) * 8 + a] = dist[
@@ -245,6 +300,9 @@
             forward(n, q).start()
         for a in range(8):
             block[n * 32 + me * 8 + a] = pool[(me * NODES + n) * 8 + a]
+
+    for load in loads:
+        load.wait()
 
     up_elem = jnp.int32(0)
     down_elem = jnp.int32(0)
@@ -520,9 +578,27 @@
         lines = lines.transpose(0, 2, 1, 3).reshape(NODES * BLOCK, 128)
         profiles = inject.reshape(4, SLAB, 128).transpose(1, 0, 2).reshape(BLOCK, 128)
         vmem = pl.BlockSpec(memory_space=pltpu.VMEM)
-        smem = pl.BlockSpec(memory_space=pltpu.SMEM)
+        hbm = pl.BlockSpec(memory_space=pltpu.HBM)
         f32 = jnp.float32
         dma = pltpu.SemaphoreType.DMA
+
+        tables = [jnp.asarray(c) for c in constants]
+        operands = [
+            lines,
+            phi.reshape(BLOCK, 128),
+            khat,
+            wall_maxw.reshape(SLAB, 128),
+            free_stream.reshape(SLAB, 128),
+            profiles,
+            *tables,
+            deriv.transpose(1, 0, 2),
+            lift.transpose(2, 0, 1),
+            normals,
+            nb_local,
+            nb_side,
+            wall_flag,
+            inj_id,
+        ]
 
         def body(*refs):
             kernel(space, *refs)
@@ -530,9 +606,11 @@
         rate = pl.pallas_call(
             body,
             out_shape=jax.ShapeDtypeStruct((NODES * BLOCK, 128), f32),
-            in_specs=[vmem] * 3 + [smem] * 3 + [vmem] * 3 + [smem] * 4 + [vmem] * 6,
+            in_specs=[hbm] * len(operands),
             out_specs=vmem,
-            scratch_shapes=[
+            scratch_shapes=[pltpu.VMEM(x.shape, x.dtype) for x in operands[:12]]
+            + [pltpu.SMEM(x.shape, x.dtype) for x in operands[12:]]
+            + [
                 pltpu.VMEM((POOL, 8, 128), f32),
                 pltpu.VMEM((NODES * 32, 8, 128), f32),
                 pltpu.VMEM((NODES * BLOCK, 128), f32),
@@ -548,6 +626,8 @@
                 pltpu.VMEM((2, 6 * 8, 8, 128), f32),
                 pltpu.VMEM((8, 128), f32),
                 pltpu.VMEM((3, 8, 128), f32),
+                dma((NODES,)),
+                dma((len(operands) - 1,)),
                 dma((NODES, 3)),
                 dma((NODES, 3)),
                 dma((NODES, 3)),
@@ -561,22 +641,7 @@
                 collective_id=0, has_side_effects=True, vmem_limit_bytes=40 * 2**20
             ),
             name="rate",
-        )(
-            lines,
-            phi.reshape(BLOCK, 128),
-            khat,
-            deriv.transpose(1, 0, 2),
-            lift.transpose(2, 0, 1),
-            normals,
-            wall_maxw.reshape(SLAB, 128),
-            free_stream.reshape(SLAB, 128),
-            profiles,
-            nb_local,
-            nb_side,
-            wall_flag,
-            inj_id,
-            *[jnp.asarray(c) for c in constants],
-        )
+        )(*operands)
         rate = rate.reshape(NODES, SLAB, ELEMS, 128).transpose(0, 2, 1, 3)
         return rate.reshape(NODES, ELEMS, SLAB * 128).transpose(1, 0, 2)
 

time: 60.5 us -> 61.3 us (1.013)
  Pallas kernels: 42.7 us -> 43.6 us
    pallas_call x1, Pallas kernels: 42.7 us -> 43.6 us  [local(): pl.pallas_call(body, out_shape=jax.ShapeDtypeStruct((NODES * BLOCK, 128),...]
where the time goes in v1:
time: 61.3 us; the launch traced here: 60.5 us
  Pallas kernels  43.6 us (71%)
  local copies, waits for them, and re-layouts  16.9 us (28%)
    pallas_call x1, Pallas kernels, local(): pl.pallas_call(body, out_shape=jax.ShapeDtypeStruct((NODES * BLOCK, 128),...  43.6 us
    unnamed x39, local copies, waits for them, and re-layouts  16.9 us

profile of v1, /device:TPU:1, one launch (start us, length us, event | category | flops | bytes accessed | tf_op | source)
XLA Modules:
  0.0 60.5 jit_solution(5296753538155067462)
XLA Ops:
  0.0 0.0 copy-start
  0.0 1.3 %copy-done = f32[4,10,8192]{2,0,1:T(4,128)S(1)} copy-done((f32[4,10,8192]{2,0,1:T(4,128)S(1)}, f32[4,10,8192]{2,0,1:T(4,128)}, u32[]{:S(2)}) %copy-start) | copy-done | bytes 1310744
  1.3 0.0 copy-start.1
  1.3 1.0 %copy-done.1 = bf16[272,768]{1,0:T(8,128)(2,1)S(1)} copy-done((bf16[272,768]{1,0:T(8,128)(2,1)S(1)}, bf16[272,768]{1,0:T(8,128)(2,1)}, u32[]{:S(2)}) %copy-start.1) | copy-done | bytes 417816
  2.3 0.0 copy-start.2
  2.3 1.0 %copy-done.2 = bf16[256,768]{1,0:T(8,128)(2,1)S(1)} copy-done((bf16[256,768]{1,0:T(8,128)(2,1)S(1)}, bf16[256,768]{1,0:T(8,128)(2,1)}, u32[]{:S(2)}) %copy-start.2) | copy-done | bytes 393240
  3.3 0.0 copy-start.3
  3.3 1.0 %copy-done.3 = bf16[768,256]{1,0:T(8,128)(2,1)S(1)} copy-done((bf16[768,256]{1,0:T(8,128)(2,1)S(1)}, bf16[768,256]{1,0:T(8,128)(2,1)}, u32[]{:S(2)}) %copy-start.3) | copy-done | bytes 393240
  4.3 0.0 copy-start.4
  4.3 1.0 %copy-done.4 = bf16[768,256]{1,0:T(8,128)(2,1)S(1)} copy-done((bf16[768,256]{1,0:T(8,128)(2,1)S(1)}, bf16[768,256]{1,0:T(8,128)(2,1)}, u32[]{:S(2)}) %copy-start.4) | copy-done | bytes 393240
  5.3 0.0 copy-start.5
  5.3 0.9 %copy-done.5 = f32[32768]{0:T(1024)S(1)} copy-done((f32[32768]{0:T(1024)S(1)}, f32[32768]{0:T(1024)}, u32[]{:S(2)}) %copy-start.5) | copy-done | bytes 131096
  6.2 0.0 copy-start.6
  6.2 0.9 %copy-done.6 = f32[32,1024]{1,0:T(8,128)S(1)} copy-done((f32[32,1024]{1,0:T(8,128)S(1)}, f32[32,1024]{1,0:T(8,128)}, u32[]{:S(2)}) %copy-start.6) | copy-done | bytes 131096
  7.1 0.0 copy-start.7
  7.1 0.9 %copy-done.7 = f32[4,8192]{1,0:T(4,128)S(1)} copy-done((f32[4,8192]{1,0:T(4,128)S(1)}, f32[4,8192]{1,0:T(4,128)}, u32[]{:S(2)}) %copy-start.7) | copy-done | bytes 131096
  8.0 0.0 copy-start.8
  8.0 0.8 %copy-done.8 = f32[8192]{0:T(1024)S(1)} copy-done((f32[8192]{0:T(1024)S(1)}, f32[8192]{0:T(1024)}, u32[]{:S(2)}) %copy-start.8) | copy-done | bytes 32792
  8.8 0.0 copy-start.9
  8.8 0.8 %copy-done.9 = f32[8192]{0:T(1024)S(1)} copy-done((f32[8192]{0:T(1024)S(1)}, f32[8192]{0:T(1024)}, u32[]{:S(2)}) %copy-start.9) | copy-done | bytes 32792
  9.5 0.0 copy-start.10
  9.5 0.8 %copy-done.10 = bf16[128,128]{1,0:T(8,128)(2,1)S(1)} copy-done((bf16[128,128]{1,0:T(8,128)(2,1)S(1)}, bf16[128,128]{1,0:T(8,128)(2,1)}, u32[]{:S(2)}) %copy-start.10) | copy-done | bytes 32792
  10.3 0.0 copy-start.11
  10.3 0.7 %copy-done.11 = f32[3,10,10]{2,0,1:T(4,128)S(1)} copy-done((f32[3,10,10]{2,0,1:T(4,128)S(1)}, f32[3,10,10]{2,0,1:T(4,128)}, u32[]{:S(2)}) %copy-start.11) | copy-done | bytes 1224
  11.0 0.0 copy-start.12
  11.0 0.7 %copy-done.12 = f32[4,10,6]{1,0,2:T(4,128)S(1)} copy-done((f32[4,10,6]{1,0,2:T(4,128)S(1)}, f32[4,10,6]{1,0,2:T(4,128)}, u32[]{:S(2)}) %copy-start.12) | copy-done | bytes 984
  11.7 0.0 copy-start.13
  11.7 0.7 %copy-done.13 = f32[16,128]{1,0:T(8,128)S(1)} copy-done((f32[16,128]{1,0:T(8,128)S(1)}, f32[16,128]{1,0:T(8,128)}, u32[]{:S(2)}) %copy-start.13) | copy-done | bytes 8216
  12.4 0.0 copy-start.14
  12.4 0.7 %copy-done.14 = f32[4,3]{1,0:T(4,128)S(1)} copy-done((f32[4,3]{1,0:T(4,128)S(1)}, f32[4,3]{1,0:T(4,128)}, u32[]{:S(2)}) %copy-start.14) | copy-done | bytes 72
  13.1 0.0 copy-start.15
  13.1 0.7 %copy-done.15 = s32[4,4]{1,0:T(4,128)S(1)} copy-done((s32[4,4]{1,0:T(4,128)S(1)}, s32[4,4]{1,0:T(4,128)}, u32[]{:S(2)}) %copy-start.15) | copy-done | bytes 88
  13.8 0.0 copy-start.16
  13.8 0.7 %copy-done.16 = s32[4,4]{1,0:T(4,128)S(1)} copy-done((s32[4,4]{1,0:T(4,128)S(1)}, s32[4,4]{1,0:T(4,128)}, u32[]{:S(2)}) %copy-start.16) | copy-done | bytes 88
  14.5 0.0 copy-start.17
  14.5 0.7 %copy-done.17 = s32[4,4]{1,0:T(4,128)S(1)} copy-done((s32[4,4]{1,0:T(4,128)S(1)}, s32[4,4]{1,0:T(4,128)}, u32[]{:S(2)}) %copy-start.17) | copy-done | bytes 88
  15.2 0.0 copy-start.18
  15.2 0.7 %copy-done.18 = s32[4,4]{1,0:T(4,128)S(1)} copy-done((s32[4,4]{1,0:T(4,128)S(1)}, s32[4,4]{1,0:T(4,128)}, u32[]{:S(2)}) %copy-start.18) | copy-done | bytes 88
  15.8 43.6 %rate.1 = f32[2560,128]{1,0:T(8,128)S(1)} custom-call(f32[2560,128]{1,0:T(8,128)S(1)} %bitcast.25, f32[256,128]{1,0:T(8,128)S(1)} %bitcast.26, f32[32,1024]{1,0:T(8,128)S(1)} %copy-done.6, f32[64,128]{1,0:T(8,128)S(1)} %bitcast.28, f32[64,128]{1,0:T(8,128)S(1)} %bitcast.29, f32[256,128]{1,0:T(8,128)S(1)} %bitcast.27, bf16[272,768]{1,0:T(8,128)(2,1)S(1)} %copy-done.1, ...), custom_call_target="tpu_custom_call" | custom-call | tf_op jit(solution)/shard_map/rate/pallas_call | solution.py:606
  59.4 1.1 %copy.23 = f32[4,10,8192]{2,0,1:T(4,128)} copy(f32[4,10,8192]{2,0,1:T(4,128)S(1)} %bitcast.24) | data formatting | bytes 2621440
Async XLA Ops:
  0.0 1.3 %copy-start = (f32[4,10,8192]{2,0,1:T(4,128)S(1)}, f32[4,10,8192]{2,0,1:T(4,128)}, u32[]{:S(2)}) copy-start(f32[4,10,8192]{2,0,1:T(4,128)} %param.19) | copy-start | bytes 3932164
  1.3 1.0 %copy-start.1 = (bf16[272,768]{1,0:T(8,128)(2,1)S(1)}, bf16[272,768]{1,0:T(8,128)(2,1)}, u32[]{:S(2)}) copy-start(bf16[272,768]{1,0:T(8,128)(2,1)} %constant.12.clone.refs_6_) | copy-start | bytes 1253380
  2.3 1.0 %copy-start.2 = (bf16[256,768]{1,0:T(8,128)(2,1)S(1)}, bf16[256,768]{1,0:T(8,128)(2,1)}, u32[]{:S(2)}) copy-start(bf16[256,768]{1,0:T(8,128)(2,1)} %constant.15.clone.refs_9_) | copy-start | bytes 1179652
  3.3 1.0 %copy-start.3 = (bf16[768,256]{1,0:T(8,128)(2,1)S(1)}, bf16[768,256]{1,0:T(8,128)(2,1)}, u32[]{:S(2)}) copy-start(bf16[768,256]{1,0:T(8,128)(2,1)} %constant.14.clone.refs_8_) | copy-start | bytes 1179652
  4.3 1.0 %copy-start.4 = (bf16[768,256]{1,0:T(8,128)(2,1)S(1)}, bf16[768,256]{1,0:T(8,128)(2,1)}, u32[]{:S(2)}) copy-start(bf16[768,256]{1,0:T(8,128)(2,1)} %constant.13.clone.refs_7_) | copy-start | bytes 1179652
  5.3 0.9 %copy-start.5 = (f32[32768]{0:T(1024)S(1)}, f32[32768]{0:T(1024)}, u32[]{:S(2)}) copy-start(f32[32768]{0:T(1024)} %param.20) | copy-start | bytes 393220
  6.2 0.9 %copy-start.6 = (f32[32,1024]{1,0:T(8,128)S(1)}, f32[32,1024]{1,0:T(8,128)}, u32[]{:S(2)}) copy-start(f32[32,1024]{1,0:T(8,128)} %refs_2_.1) | copy-start | bytes 393220
  7.1 0.9 %copy-start.7 = (f32[4,8192]{1,0:T(4,128)S(1)}, f32[4,8192]{1,0:T(4,128)}, u32[]{:S(2)}) copy-start(f32[4,8192]{1,0:T(4,128)} %param.27) | copy-start | bytes 393220
  8.0 0.8 %copy-start.8 = (f32[8192]{0:T(1024)S(1)}, f32[8192]{0:T(1024)}, u32[]{:S(2)}) copy-start(f32[8192]{0:T(1024)} %param.25) | copy-start | bytes 98308
  8.8 0.8 %copy-start.9 = (f32[8192]{0:T(1024)S(1)}, f32[8192]{0:T(1024)}, u32[]{:S(2)}) copy-start(f32[8192]{0:T(1024)} %param.26) | copy-start | bytes 98308
  9.5 0.8 %copy-start.10 = (bf16[128,128]{1,0:T(8,128)(2,1)S(1)}, bf16[128,128]{1,0:T(8,128)(2,1)}, u32[]{:S(2)}) copy-start(bf16[128,128]{1,0:T(8,128)(2,1)} %constant.17.clone.refs_11_) | copy-start | bytes 98308
  10.3 0.7 %copy-start.11 = (f32[3,10,10]{2,0,1:T(4,128)S(1)}, f32[3,10,10]{2,0,1:T(4,128)}, u32[]{:S(2)}) copy-start(f32[3,10,10]{2,0,1:T(4,128)} %param.22) | copy-start | bytes 3604
  11.0 0.7 %copy-start.12 = (f32[4,10,6]{1,0,2:T(4,128)S(1)}, f32[4,10,6]{1,0,2:T(4,128)}, u32[]{:S(2)}) copy-start(f32[4,10,6]{1,0,2:T(4,128)} %param.23) | copy-start | bytes 2884
  11.7 0.7 %copy-start.13 = (f32[16,128]{1,0:T(8,128)S(1)}, f32[16,128]{1,0:T(8,128)}, u32[]{:S(2)}) copy-start(f32[16,128]{1,0:T(8,128)} %constant.16.clone.refs_10_) | copy-start | bytes 24580
  12.4 0.7 %copy-start.14 = (f32[4,3]{1,0:T(4,128)S(1)}, f32[4,3]{1,0:T(4,128)}, u32[]{:S(2)}) copy-start(f32[4,3]{1,0:T(4,128)} %refs_14_.1) | copy-start | bytes 148
  13.1 0.7 %copy-start.15 = (s32[4,4]{1,0:T(4,128)S(1)}, s32[4,4]{1,0:T(4,128)}, u32[]{:S(2)}) copy-start(s32[4,4]{1,0:T(4,128)} %refs_15_.1) | copy-start | bytes 196
  13.8 0.7 %copy-start.16 = (s32[4,4]{1,0:T(4,128)S(1)}, s32[4,4]{1,0:T(4,128)}, u32[]{:S(2)}) copy-start(s32[4,4]{1,0:T(4,128)} %refs_16_.1) | copy-start | bytes 196
  14.5 0.7 %copy-start.17 = (s32[4,4]{1,0:T(4,128)S(1)}, s32[4,4]{1,0:T(4,128)}, u32[]{:S(2)}) copy-start(s32[4,4]{1,0:T(4,128)} %refs_17_.1) | copy-start | bytes 196
  15.2 0.7 %copy-start.18 = (s32[4,4]{1,0:T(4,128)S(1)}, s32[4,4]{1,0:T(4,128)}, u32[]{:S(2)}) copy-start(s32[4,4]{1,0:T(4,128)} %refs_18_.1) | copy-start | bytes 196

commit v2 on v1

--- a/solution.py
+++ b/solution.py
@@ -151,6 +151,7 @@
     nb_side_in,
     wall_flag_in,
     inj_id_in,
+    out_hbm,
     out,
     dist,
     phi,
@@ -187,6 +188,7 @@
     sums_out,
     sums_in,
     dist_sem,
+    out_sem,
     load_sem,
     fwd_send,
     fwd_recv,
@@ -251,6 +253,10 @@
     def dist_load(n):
         part = rows(n * BLOCK, BLOCK)
         return pltpu.make_async_copy(dist_in.at[part], dist.at[part], dist_sem.at[n])
+
+    def store(n):
+        part = rows(n * BLOCK, BLOCK)
+        return pltpu.make_async_copy(out.at[part], out_hbm.at[part], out_sem.at[n])
 
     pairs = (
         (nb_side_in, nb_side),
@@ -522,12 +528,14 @@
             for a in range(8):
                 at = rows((e * NODES + n) * SLAB + a * 8)
                 out[pl.ds(n * BLOCK + a * 32 + e, 8, stride=4), :] = back[at, :] + moved[at, :]
+        store(n).start()
 
     @pl.loop(0, NODES)
     def _(n):
         for q in range(3):
             forward(n, q).wait_send()
             backward(n, q).wait_send()
+        store(n).wait()
 
     for side in range(2):
         halo(side).wait_send()
@@ -577,7 +585,6 @@
         lines = dist.transpose(1, 0, 2).reshape(NODES, ELEMS, SLAB, 128)
         lines = lines.transpose(0, 2, 1, 3).reshape(NODES * BLOCK, 128)
         profiles = inject.reshape(4, SLAB, 128).transpose(1, 0, 2).reshape(BLOCK, 128)
-        vmem = pl.BlockSpec(memory_space=pltpu.VMEM)
         hbm = pl.BlockSpec(memory_space=pltpu.HBM)
         f32 = jnp.float32
         dma = pltpu.SemaphoreType.DMA
@@ -607,8 +614,9 @@
             body,
             out_shape=jax.ShapeDtypeStruct((NODES * BLOCK, 128), f32),
             in_specs=[hbm] * len(operands),
-            out_specs=vmem,
-            scratch_shapes=[pltpu.VMEM(x.shape, x.dtype) for x in operands[:12]]
+            out_specs=hbm,
+            scratch_shapes=[pltpu.VMEM((NODES * BLOCK, 128), f32)]
+            + [pltpu.VMEM(x.shape, x.dtype) for x in operands[:12]]
             + [pltpu.SMEM(x.shape, x.dtype) for x in operands[12:]]
             + [
                 pltpu.VMEM((POOL, 8, 128), f32),
@@ -627,6 +635,7 @@
                 pltpu.VMEM((8, 128), f32),
                 pltpu.VMEM((3, 8, 128), f32),
                 dma((NODES,)),
+                dma((NODES,)),
                 dma((len(operands) - 1,)),
                 dma((NODES, 3)),
                 dma((NODES, 3)),
@@ -638,7 +647,7 @@
                 dma((3,)),
             ],
             compiler_params=pltpu.CompilerParams(
-                collective_id=0, has_side_effects=True, vmem_limit_bytes=40 * 2**20
+                collective_id=0, has_side_effects=True, vmem_limit_bytes=60 * 2**20
             ),
             name="rate",
         )(*operands)

time: 61.3 us -> 44.9 us (0.73); the launches traced: 60.5 us -> 44.7 us
  local copies, waits for them, and re-layouts: 16.9 us -> 2.47 us
  Pallas kernels: 43.6 us -> 42.3 us
    unnamed x39 -> x1, local copies, waits for them, and re-layouts: 16.9 us -> 2.47 us
    pallas_call x1, Pallas kernels: 43.6 us -> 42.3 us  [local(): pl.pallas_call(body, out_shape=jax.ShapeDtypeStruct((NODES * BLOCK, 128),...]
where the time goes in v2:
time: 44.9 us; the launch traced here: 44.7 us
  Pallas kernels  42.3 us (94%)
  local copies, waits for them, and re-layouts  2.47 us (6%)
    pallas_call x1, Pallas kernels, local(): pl.pallas_call(body, out_shape=jax.ShapeDtypeStruct((NODES * BLOCK, 128),...  42.3 us
    unnamed x1, local copies, waits for them, and re-layouts  2.47 us

profile of v2, /device:TPU:1, one launch (start us, length us, event | category | flops | bytes accessed | tf_op | source)
XLA Modules:
  0.0 44.7 jit_solution(11476511016501382554)
XLA Ops:
  0.0 42.3 %rate.1 = f32[2560,128]{1,0:T(8,128)} custom-call(f32[2560,128]{1,0:T(8,128)} %bitcast.25, f32[256,128]{1,0:T(8,128)} %bitcast.26, f32[32,1024]{1,0:T(8,128)} %refs_2_.1, f32[64,128]{1,0:T(8,128)} %bitcast.28, f32[64,128]{1,0:T(8,128)} %bitcast.29, f32[256,128]{1,0:T(8,128)} %bitcast.27, bf16[272,768]{1,0:T(8,128)(2,1)} %constant.12.clone.refs_6_, ...), custom_call_target="tpu_custom_call" | custom-call | tf_op jit(solution)/shard_map/rate/pallas_call | solution.py:613
  42.3 2.5 %copy.23 = f32[4,10,8192]{2,0,1:T(4,128)} copy(f32[4,10,8192]{2,0,1:T(4,128)} %bitcast.24) | data formatting | bytes 2621440

commit v3 on v2

--- a/solution.py
+++ b/solution.py
@@ -202,8 +202,10 @@
     f32 = jnp.float32
     me = lax.axis_index("vel")
     here = lax.axis_index("space")
-    above = lax.rem(here + 1, space)
-    below = lax.rem(here + space - 1, space)
+    parity = lax.rem(here, 2)
+    has_above = here < space - 1
+    has_below = here > 0
+    beside = jnp.where(has_above, 1, 0) + jnp.where(has_below, 1, 0)
     core = lax.rem(me, 2)
     flip = 1 - 2 * core
     across = lax.rem(me + 2, GROUP)
@@ -238,7 +240,7 @@
             dst_ref=halo_in.at[side],
             send_sem=halo_send.at[side],
             recv_sem=halo_recv.at[side],
-            device_id={"space": below if side else above},
+            device_id={"space": lax.rem(here + (space - 1 if side else 1), space)},
         )
 
     def sums(q):
@@ -286,13 +288,29 @@
     barrier = pltpu.get_barrier_semaphore()
     for to in partners:
         pl.semaphore_signal(barrier, inc=1, device_id={"vel": to})
-    for to in (above, below):
-        pl.semaphore_signal(barrier, inc=1, device_id={"space": to})
     for n in range(NODES):
         dist_load(n).start()
+
+    def greet():
+        @pl.when(has_above)
+        def _():
+            pl.semaphore_signal(barrier, inc=1, device_id={"space": here + 1})
+
+        @pl.when(has_below)
+        def _():
+            pl.semaphore_signal(barrier, inc=1, device_id={"space": here - 1})
+
+    @pl.when(parity == 1)
+    def _():
+        pl.semaphore_wait(barrier, 3 + beside)
+
+    @pl.when(parity == 0)
+    def _():
+        pl.semaphore_wait(barrier, 3)
+
+    greet()
     for load in loads:
         load.start()
-    pl.semaphore_wait(barrier, 5)
 
     @pl.loop(0, NODES)
     def _(n):
@@ -309,17 +327,6 @@
 
     for load in loads:
         load.wait()
-
-    up_elem = jnp.int32(0)
-    down_elem = jnp.int32(0)
-    for e in range(ELEMS):
-        up_elem = up_elem + jnp.where(nb_side[e, 1] == 2, e, 0)
-        down_elem = down_elem + jnp.where(nb_side[e, 0] == 1, e, 0)
-    for side, elem, face in ((0, up_elem, 1), (1, down_elem, 0)):
-        for k in range(6):
-            for a in range(8):
-                halo_out[side, k * 8 + a] = pool[(elem * NODES + FACES[face][k]) * 8 + a]
-        halo(side).start()
 
     for q in range(4):
         for a in range(8):
@@ -412,12 +419,60 @@
             moved[ka * 8 : ka * 8 + 8, :] + moved[other : other + 8, :]
         )
 
+    def send_halos():
+        @pl.when(parity == 0)
+        def _():
+            pl.semaphore_wait(barrier, beside)
+
+
+        up_elem = jnp.int32(0)
+        down_elem = jnp.int32(0)
+        for e in range(ELEMS):
+            up_elem = up_elem + jnp.where(nb_side[e, 1] == 2, e, 0)
+            down_elem = down_elem + jnp.where(nb_side[e, 0] == 1, e, 0)
+        for side, elem, face in ((0, up_elem, 1), (1, down_elem, 0)):
+            for k in range(6):
+                for a in range(8):
+                    halo_out[side, k * 8 + a] = pool[(elem * NODES + FACES[face][k]) * 8 + a]
+
+            @pl.when(has_below if side else has_above)
+            def _():
+                halo(side).start()
+
+    cos = twiddle[0:8, :]
+    sin = twiddle[8:16, :]
+
+    @pl.loop(0, NODES)
+    def _(n):
+        @pl.when(n == 3)
+        def _():
+            send_halos()
+
+        for q in range(3):
+            forward_in(n, q, block, pool, fwd_send, fwd_recv, partners, rows).wait_recv()
+        result[rows(n * BLOCK, BLOCK), :] = collide(
+            block[pl.ds(n * 32, 32)].reshape(BLOCK, 128),
+            phi[...],
+            sym[...],
+            rows_fwd[...],
+            lanes_fwd[...],
+            lanes_bwd[...],
+            rows_bwd[...],
+            cos,
+            sin,
+        )
+        for q in range(3):
+            backward(n, q).start()
+
     for side, face in ((0, 1), (1, 0)):
-        halo(side).wait_recv()
-        for k in range(6):
-            start = HALO + (side * NODES + FACES[face][k]) * 8
-            for a in range(8):
-                pool[start + a] = halo_in[side, k * 8 + a]
+
+        @pl.when(has_above if side else has_below)
+        def _():
+            halo(side).wait_recv()
+            for k in range(6):
+                start = HALO + (side * NODES + FACES[face][k]) * 8
+                for a in range(8):
+                    pool[start + a] = halo_in[side, k * 8 + a]
 
     @pl.loop(0, 8)
     def _(a):
@@ -459,27 +514,6 @@
                 for e in range(ELEMS):
                     moved[rows((e * NODES + pair * 2 + i) * SLAB + a * 8), :] = acc[i][e]
 
-    cos = twiddle[0:8, :]
-    sin = twiddle[8:16, :]
-
-    @pl.loop(0, NODES)
-    def _(n):
-        for q in range(3):
-            forward_in(n, q, block, pool, fwd_send, fwd_recv, partners, rows).wait_recv()
-        result[rows(n * BLOCK, BLOCK), :] = collide(
-            block[pl.ds(n * 32, 32)].reshape(BLOCK, 128),
-            phi[...],
-            sym[...],
-            rows_fwd[...],
-            lanes_fwd[...],
-            lanes_bwd[...],
-            rows_bwd[...],
-            cos,
-            sin,
-        )
-        for q in range(3):
-            backward(n, q).start()
-
     total = sums_out[...]
     for q in range(3):
         sums(q).wait_recv()
@@ -538,7 +572,11 @@
         store(n).wait()
 
     for side in range(2):
-        halo(side).wait_send()
+
+        @pl.when(has_below if side else has_above)
+        def _():
+            halo(side).wait_send()
+
     for q in range(3):
         sums(q).wait_send()
 

time: 44.9 us -> 42.9 us (0.955)
  the two profiles are of different devices: /device:TPU:1 before, /device:TPU:47 now
where the time goes in v3:
time: 42.9 us; the launch traced here: 42.7 us
  Pallas kernels  40.2 us (94%)
  local copies, waits for them, and re-layouts  2.47 us (6%)
    pallas_call x1, Pallas kernels, local(): pl.pallas_call(body, out_shape=jax.ShapeDtypeStruct((NODES * BLOCK, 128),...  40.2 us
    unnamed x1, local copies, waits for them, and re-layouts  2.47 us

profile of v3, /device:TPU:47, one launch (start us, length us, event | category | flops | bytes accessed | tf_op | source)
XLA Modules:
  0.0 42.7 jit_solution(174576138941235150)
XLA Ops:
  0.0 40.2 %rate.1 = f32[2560,128]{1,0:T(8,128)} custom-call(f32[2560,128]{1,0:T(8,128)} %bitcast.25, f32[256,128]{1,0:T(8,128)} %bitcast.26, f32[32,1024]{1,0:T(8,128)} %refs_2_.1, f32[64,128]{1,0:T(8,128)} %bitcast.28, f32[64,128]{1,0:T(8,128)} %bitcast.29, f32[256,128]{1,0:T(8,128)} %bitcast.27, bf16[272,768]{1,0:T(8,128)(2,1)} %constant.12.clone.refs_6_, ...), custom_call_target="tpu_custom_call" | custom-call | tf_op jit(solution)/shard_map/rate/pallas_call | solution.py:651
  40.2 2.5 %copy.23 = f32[4,10,8192]{2,0,1:T(4,128)} copy(f32[4,10,8192]{2,0,1:T(4,128)} %bitcast.24) | data formatting | bytes 2621440

commit v4 on v3

--- a/solution.py
+++ b/solution.py
@@ -151,7 +151,6 @@
     nb_side_in,
     wall_flag_in,
     inj_id_in,
-    out_hbm,
     out,
     dist,
     phi,
@@ -188,7 +187,6 @@
     sums_out,
     sums_in,
     dist_sem,
-    out_sem,
     load_sem,
     fwd_send,
     fwd_recv,
@@ -255,10 +253,6 @@
     def dist_load(n):
         part = rows(n * BLOCK, BLOCK)
         return pltpu.make_async_copy(dist_in.at[part], dist.at[part], dist_sem.at[n])
-
-    def store(n):
-        part = rows(n * BLOCK, BLOCK)
-        return pltpu.make_async_copy(out.at[part], out_hbm.at[part], out_sem.at[n])
 
     pairs = (
         (nb_side_in, nb_side),
@@ -290,6 +284,8 @@
         pl.semaphore_signal(barrier, inc=1, device_id={"vel": to})
     for n in range(NODES):
         dist_load(n).start()
+    for load in loads:
+        load.start()
 
     def greet():
         @pl.when(has_above)
@@ -309,8 +305,6 @@
         pl.semaphore_wait(barrier, 3)
 
     greet()
-    for load in loads:
-        load.start()
 
     @pl.loop(0, NODES)
     def _(n):
@@ -562,14 +556,12 @@
             for a in range(8):
                 at = rows((e * NODES + n) * SLAB + a * 8)
                 out[pl.ds(n * BLOCK + a * 32 + e, 8, stride=4), :] = back[at, :] + moved[at, :]
-        store(n).start()
 
     @pl.loop(0, NODES)
     def _(n):
         for q in range(3):
             forward(n, q).wait_send()
             backward(n, q).wait_send()
-        store(n).wait()
 
     for side in range(2):
 
@@ -652,9 +644,8 @@
             body,
             out_shape=jax.ShapeDtypeStruct((NODES * BLOCK, 128), f32),
             in_specs=[hbm] * len(operands),
-            out_specs=hbm,
-            scratch_shapes=[pltpu.VMEM((NODES * BLOCK, 128), f32)]
-            + [pltpu.VMEM(x.shape, x.dtype) for x in operands[:12]]
+            out_specs=pl.BlockSpec(memory_space=pltpu.VMEM),
+            scratch_shapes=[pltpu.VMEM(x.shape, x.dtype) for x in operands[:12]]
             + [pltpu.SMEM(x.shape, x.dtype) for x in operands[12:]]
             + [
                 pltpu.VMEM((POOL, 8, 128), f32),
@@ -673,7 +664,6 @@
                 pltpu.VMEM((8, 128), f32),
                 pltpu.VMEM((3, 8, 128), f32),
                 dma((NODES,)),
-                dma((NODES,)),
                 dma((len(operands) - 1,)),
                 dma((NODES, 3)),
                 dma((NODES, 3)),
@@ -685,10 +675,10 @@
                 dma((3,)),
             ],
             compiler_params=pltpu.CompilerParams(
-                collective_id=0, has_side_effects=True, vmem_limit_bytes=60 * 2**20
+                collective_id=0, has_side_effects=True, vmem_limit_bytes=40 * 2**20
             ),
             name="rate",
-        )(*operands)
+        )(*[pltpu.with_memory_space_constraint(x, pltpu.HBM) for x in operands])
         rate = rate.reshape(NODES, SLAB, ELEMS, 128).transpose(0, 2, 1, 3)
         return rate.reshape(NODES, ELEMS, SLAB * 128).transpose(1, 0, 2)
 

time: 42.9 us -> 40.8 us (0.951)
  local copies, waits for them, and re-layouts: 2.47 us -> 1.06 us
  Pallas kernels: 40.2 us -> 39.6 us
    unnamed x1, local copies, waits for them, and re-layouts: 2.47 us -> 1.06 us
    pallas_call x1, Pallas kernels: 40.2 us -> 39.6 us  [local(): pl.pallas_call(body, out_shape=jax.ShapeDtypeStruct((NODES * BLOCK, 128),...]
where the time goes in v4:
time: 40.8 us; the launch traced here: 40.7 us
  Pallas kernels  39.6 us (97%)
  local copies, waits for them, and re-layouts  1.06 us (3%)
    pallas_call x1, Pallas kernels, local(): pl.pallas_call(body, out_shape=jax.ShapeDtypeStruct((NODES * BLOCK, 128),...  39.6 us
    unnamed x1, local copies, waits for them, and re-layouts  1.06 us

profile of v4, /device:TPU:47, one launch (start us, length us, event | category | flops | bytes accessed | tf_op | source)
XLA Modules:
  0.0 40.7 jit_solution(9148197630801255689)
XLA Ops:
  0.0 39.6 %rate.1 = f32[2560,128]{1,0:T(8,128)S(1)} custom-call(f32[2560,128]{1,0:T(8,128)} %bitcast.25, f32[256,128]{1,0:T(8,128)} %bitcast.26, f32[32,1024]{1,0:T(8,128)} %refs_2_.1, f32[64,128]{1,0:T(8,128)} %bitcast.28, f32[64,128]{1,0:T(8,128)} %bitcast.29, f32[256,128]{1,0:T(8,128)} %bitcast.27, bf16[272,768]{1,0:T(8,128)(2,1)} %constant.12.clone.refs_6_, ...), custom_call_target="tpu_custom_call" | custom-call | tf_op jit(solution)/shard_map/rate/pallas_call | solution.py:643
  39.6 1.1 %copy.23 = f32[4,10,8192]{2,0,1:T(4,128)} copy(f32[4,10,8192]{2,0,1:T(4,128)S(1)} %bitcast.24) | data formatting | bytes 2621440

commit v5 on v4

--- a/solution.py
+++ b/solution.py
@@ -21,6 +21,8 @@
 TABLE = ELEMS * NODES * 8
 HALO = TABLE + 5 * 8
 POOL = HALO + 2 * NODES * 8
+LINE = 4
+DIRECT = (24, 16)
 
 
 def split(x):
@@ -184,6 +186,7 @@
     wallsum,
     halo_out,
     halo_in,
+    relay,
     sums_out,
     sums_in,
     dist_sem,
@@ -194,6 +197,9 @@
     bwd_recv,
     halo_send,
     halo_recv,
+    relay_send,
+    relay_recv,
+    relay_ready,
     sums_send,
     sums_recv,
 ):
@@ -203,6 +209,11 @@
     parity = lax.rem(here, 2)
     has_above = here < space - 1
     has_below = here > 0
+    place = lax.rem(here, LINE)
+    turn_up = (place == LINE - 1) & has_above
+    turn_down = (place == 0) & has_below
+    relay_up = (place == 1) & (here > LINE)
+    relay_down = (place == LINE - 2) & (here < space - LINE)
     beside = jnp.where(has_above, 1, 0) + jnp.where(has_below, 1, 0)
     core = lax.rem(me, 2)
     flip = 1 - 2 * core
@@ -232,13 +243,33 @@
             device_id={"vel": to},
         )
 
-    def halo(side):
+    def halo(side, count=48):
         return pltpu.make_async_remote_copy(
-            src_ref=halo_out.at[side],
-            dst_ref=halo_in.at[side],
+            src_ref=halo_out.at[side, pl.ds(0, count)],
+            dst_ref=halo_in.at[side, pl.ds(0, count)],
             send_sem=halo_send.at[side],
             recv_sem=halo_recv.at[side],
             device_id={"space": lax.rem(here + (space - 1 if side else 1), space)},
+        )
+
+    def detour(side):
+        first = DIRECT[side]
+        return pltpu.make_async_remote_copy(
+            src_ref=halo_out.at[side, pl.ds(first, 48 - first)],
+            dst_ref=relay.at[pl.ds(0, 48 - first)],
+            send_sem=relay_send.at[0],
+            recv_sem=relay_recv.at[0],
+            device_id={"space": lax.rem(here + (space - 2 if side else 2), space)},
+        )
+
+    def passed(side):
+        first = DIRECT[side]
+        return pltpu.make_async_remote_copy(
+            src_ref=relay.at[pl.ds(0, 48 - first)],
+            dst_ref=halo_in.at[side, pl.ds(first, 48 - first)],
+            send_sem=relay_send.at[1],
+            recv_sem=relay_recv.at[1],
+            device_id={"space": lax.rem(here + (1 if side else space - 1), space)},
         )
 
     def sums(q):
@@ -418,6 +449,13 @@
         def _():
             pl.semaphore_wait(barrier, beside)
 
+        @pl.when(turn_down)
+        def _():
+            pl.semaphore_signal(relay_ready, inc=1, device_id={"space": here - 1})
+
+        @pl.when(turn_up)
+        def _():
+            pl.semaphore_signal(relay_ready, inc=1, device_id={"space": here + 1})
 
         up_elem = jnp.int32(0)
         down_elem = jnp.int32(0)
@@ -429,9 +467,18 @@
                 for a in range(8):
                     halo_out[side, k * 8 + a] = pool[(elem * NODES + FACES[face][k]) * 8 + a]
 
-            @pl.when(has_below if side else has_above)
+            turn = turn_down if side else turn_up
+            straight_on = (has_below if side else has_above) & jnp.logical_not(turn)
+
+            @pl.when(straight_on)
             def _():
                 halo(side).start()
+
+            @pl.when(turn)
+            def _():
+                halo(side, DIRECT[side]).start()
+                pl.semaphore_wait(relay_ready, 1)
+                detour(side).start()
 
     cos = twiddle[0:8, :]
     sin = twiddle[8:16, :]
@@ -458,11 +505,50 @@
         for q in range(3):
             backward(n, q).start()
 
+    for side in range(2):
+
+        @pl.when(relay_down if side else relay_up)
+        def _():
+            detour(side).wait_recv()
+            passed(side).start()
+
+    total = sums_out[...]
+    for q in range(3):
+        sums(q).wait_recv()
+    for q in range(3):
+        total = total + sums_in[q]
+    for j in range(4):
+        mask = zero
+        for e in range(ELEMS):
+            on = jnp.where(nb_side[e, j] == 3, jnp.where(wall_flag[e, j] == 1, 1.0, 0.0), 0.0)
+            mask = jnp.where(sub % 4 == e, on, mask)
+        den = jnp.broadcast_to(total[:, 24 + j : 25 + j], (8, 128))
+        sigma = [
+            jnp.broadcast_to(total[:, j * 6 + k : j * 6 + k + 1], (8, 128)) / den * mask
+            for k in range(6)
+        ]
+        for n in range(NODES):
+            part = lift[0, j, n] * sigma[0]
+            for k in range(1, 6):
+                part = part + lift[k, j, n] * sigma[k]
+            wallsum[(j * NODES + n) * 8 : (j * NODES + n) * 8 + 8, :] = part
+
     for side, face in ((0, 1), (1, 0)):
 
-        @pl.when(has_above if side else has_below)
+        turn = turn_up if side else turn_down
+        here_in = has_above if side else has_below
+
+        @pl.when(here_in & jnp.logical_not(turn))
         def _():
             halo(side).wait_recv()
+
+        @pl.when(turn)
+        def _():
+            halo(side, DIRECT[side]).wait_recv()
+            passed(side).wait_recv()
+
+        @pl.when(here_in)
+        def _():
             for k in range(6):
                 start = HALO + (side * NODES + FACES[face][k]) * 8
                 for a in range(8):
@@ -508,27 +594,6 @@
                 for e in range(ELEMS):
                     moved[rows((e * NODES + pair * 2 + i) * SLAB + a * 8), :] = acc[i][e]
 
-    total = sums_out[...]
-    for q in range(3):
-        sums(q).wait_recv()
-    for q in range(3):
-        total = total + sums_in[q]
-    for j in range(4):
-        mask = zero
-        for e in range(ELEMS):
-            on = jnp.where(nb_side[e, j] == 3, jnp.where(wall_flag[e, j] == 1, 1.0, 0.0), 0.0)
-            mask = jnp.where(sub % 4 == e, on, mask)
-        den = jnp.broadcast_to(total[:, 24 + j : 25 + j], (8, 128))
-        sigma = [
-            jnp.broadcast_to(total[:, j * 6 + k : j * 6 + k + 1], (8, 128)) / den * mask
-            for k in range(6)
-        ]
-        for n in range(NODES):
-            part = lift[0, j, n] * sigma[0]
-            for k in range(1, 6):
-                part = part + lift[k, j, n] * sigma[k]
-            wallsum[(j * NODES + n) * 8 : (j * NODES + n) * 8 + 8, :] = part
-
     @pl.loop(0, ELEMS)
     def _(e):
         @pl.loop(0, NODES)
@@ -564,10 +629,21 @@
             backward(n, q).wait_send()
 
     for side in range(2):
-
-        @pl.when(has_below if side else has_above)
+        turn = turn_down if side else turn_up
+        straight_on = (has_below if side else has_above) & jnp.logical_not(turn)
+
+        @pl.when(straight_on)
         def _():
             halo(side).wait_send()
+
+        @pl.when(turn)
+        def _():
+            halo(side, DIRECT[side]).wait_send()
+            detour(side).wait_send()
+
+        @pl.when(relay_down if side else relay_up)
+        def _():
+            passed(side).wait_send()
 
     for q in range(3):
         sums(q).wait_send()
@@ -661,6 +737,7 @@
                 pltpu.VMEM((4 * NODES * 8, 128), f32),
                 pltpu.VMEM((2, 6 * 8, 8, 128), f32),
                 pltpu.VMEM((2, 6 * 8, 8, 128), f32),
+                pltpu.VMEM((6 * 8, 8, 128), f32),
                 pltpu.VMEM((8, 128), f32),
                 pltpu.VMEM((3, 8, 128), f32),
                 dma((NODES,)),
@@ -671,6 +748,9 @@
                 dma((NODES, 3)),
                 dma((2,)),
                 dma((2,)),
+                dma((2,)),
+                dma((2,)),
+                pltpu.SemaphoreType.REGULAR,
                 dma((3,)),
                 dma((3,)),
             ],

time: 40.8 us -> 38 us (0.931)
  the two profiles are of different devices: /device:TPU:47 before, /device:TPU:79 now
where the time goes in v5:
time: 38 us; the launch traced here: 37.9 us
  Pallas kernels  36.8 us (97%)
  local copies, waits for them, and re-layouts  1.06 us (3%)
    pallas_call x1, Pallas kernels, local(): pl.pallas_call(body, out_shape=jax.ShapeDtypeStruct((NODES * BLOCK, 128),...  36.8 us
    unnamed x1, local copies, waits for them, and re-layouts  1.06 us

profile of v5, /device:TPU:79, one launch (start us, length us, event | category | flops | bytes accessed | tf_op | source)
XLA Modules:
  0.0 37.9 jit_solution(9172275235021722966)
XLA Ops:
  0.0 36.8 %rate.1 = f32[2560,128]{1,0:T(8,128)S(1)} custom-call(f32[2560,128]{1,0:T(8,128)} %bitcast.25, f32[256,128]{1,0:T(8,128)} %bitcast.26, f32[32,1024]{1,0:T(8,128)} %refs_2_.1, f32[64,128]{1,0:T(8,128)} %bitcast.28, f32[64,128]{1,0:T(8,128)} %bitcast.29, f32[256,128]{1,0:T(8,128)} %bitcast.27, bf16[272,768]{1,0:T(8,128)(2,1)} %constant.12.clone.refs_6_, ...), custom_call_target="tpu_custom_call" | custom-call | tf_op jit(solution)/shard_map/rate/pallas_call | solution.py:719
  36.8 1.1 %copy.23 = f32[4,10,8192]{2,0,1:T(4,128)} copy(f32[4,10,8192]{2,0,1:T(4,128)S(1)} %bitcast.24) | data formatting | bytes 2621440

commit v6 on v5

--- a/solution.py
+++ b/solution.py
@@ -22,7 +22,7 @@
 HALO = TABLE + 5 * 8
 POOL = HALO + 2 * NODES * 8
 LINE = 4
-DIRECT = (24, 16)
+DIRECT = (24, 24)
 
 
 def split(x):
@@ -206,7 +206,6 @@
     f32 = jnp.float32
     me = lax.axis_index("vel")
     here = lax.axis_index("space")
-    parity = lax.rem(here, 2)
     has_above = here < space - 1
     has_below = here > 0
     place = lax.rem(here, LINE)
@@ -216,6 +215,7 @@
     relay_down = (place == LINE - 2) & (here < space - LINE)
     beside = jnp.where(has_above, 1, 0) + jnp.where(has_below, 1, 0)
     core = lax.rem(me, 2)
+    parity = lax.rem(here + core + 1, 2)
     flip = 1 - 2 * core
     across = lax.rem(me + 2, GROUP)
     partners = (across, across + flip, me + flip)
@@ -480,6 +480,14 @@
                 pl.semaphore_wait(relay_ready, 1)
                 detour(side).start()
 
+    def pass_on():
+        for side in range(2):
+
+            @pl.when(relay_down if side else relay_up)
+            def _():
+                detour(side).wait_recv()
+                passed(side).start()
+
     cos = twiddle[0:8, :]
     sin = twiddle[8:16, :]
 
@@ -488,6 +496,10 @@
         @pl.when(n == 3)
         def _():
             send_halos()
+
+        @pl.when(n == 9)
+        def _():
+            pass_on()
 
         for q in range(3):
             forward_in(n, q, block, pool, fwd_send, fwd_recv, partners, rows).wait_recv()
@@ -504,13 +516,6 @@
         )
         for q in range(3):
             backward(n, q).start()
-
-    for side in range(2):
-
-        @pl.when(relay_down if side else relay_up)
-        def _():
-            detour(side).wait_recv()
-            passed(side).start()
 
     total = sums_out[...]
     for q in range(3):

time: 38 us -> 37.6 us (0.989)
  the two profiles are of different devices: /device:TPU:79 before, /device:TPU:1 now
where the time goes in v6:
time: 37.6 us; the launch traced here: 37.2 us
  Pallas kernels  36.1 us (96%)
  local copies, waits for them, and re-layouts  1.06 us (3%)
    pallas_call x1, Pallas kernels, local(): pl.pallas_call(body, out_shape=jax.ShapeDtypeStruct((NODES * BLOCK, 128),...  36.1 us
    unnamed x1, local copies, waits for them, and re-layouts  1.06 us

profile of v6, /device:TPU:1, one launch (start us, length us, event | category | flops | bytes accessed | tf_op | source)
XLA Modules:
  0.0 37.2 jit_solution(11010880549607659164)
XLA Ops:
  0.0 36.1 %rate.1 = f32[2560,128]{1,0:T(8,128)S(1)} custom-call(f32[2560,128]{1,0:T(8,128)} %bitcast.25, f32[256,128]{1,0:T(8,128)} %bitcast.26, f32[32,1024]{1,0:T(8,128)} %refs_2_.1, f32[64,128]{1,0:T(8,128)} %bitcast.28, f32[64,128]{1,0:T(8,128)} %bitcast.29, f32[256,128]{1,0:T(8,128)} %bitcast.27, bf16[272,768]{1,0:T(8,128)(2,1)} %constant.12.clone.refs_6_, ...), custom_call_target="tpu_custom_call" | custom-call | tf_op jit(solution)/shard_map/rate/pallas_call | solution.py:724
  36.2 1.1 %copy.23 = f32[4,10,8192]{2,0,1:T(4,128)} copy(f32[4,10,8192]{2,0,1:T(4,128)S(1)} %bitcast.24) | data formatting | bytes 2621440

commit v7 on v6

--- a/solution.py
+++ b/solution.py
@@ -327,28 +327,38 @@
         def _():
             pl.semaphore_signal(barrier, inc=1, device_id={"space": here - 1})
 
-    @pl.when(parity == 1)
-    def _():
-        pl.semaphore_wait(barrier, 3 + beside)
-
-    @pl.when(parity == 0)
-    def _():
-        pl.semaphore_wait(barrier, 3)
-
-    greet()
-
-    @pl.loop(0, NODES)
-    def _(n):
+    def repack(n):
         dist_load(n).wait()
         for e in range(ELEMS):
             for a in range(8):
                 pool[(e * NODES + n) * 8 + a] = dist[
                     pl.ds(n * BLOCK + a * 32 + e, 8, stride=4), :
                 ]
+
+    repack(0)
+
+    @pl.when(parity == 1)
+    def _():
+        pl.semaphore_wait(barrier, 3 + beside)
+
+    @pl.when(parity == 0)
+    def _():
+        pl.semaphore_wait(barrier, 3)
+
+    greet()
+
+    def send(n):
         for q in range(3):
             forward(n, q).start()
         for a in range(8):
             block[n * 32 + me * 8 + a] = pool[(me * NODES + n) * 8 + a]
+
+    send(0)
+
+    @pl.loop(1, NODES)
+    def _(n):
+        repack(n)
+        send(n)
 
     for load in loads:
         load.wait()
@@ -516,6 +526,8 @@
         )
         for q in range(3):
             backward(n, q).start()
+        for q in range(3):
+            forward(n, q).wait_send()
 
     total = sums_out[...]
     for q in range(3):
@@ -626,11 +638,7 @@
             for a in range(8):
                 at = rows((e * NODES + n) * SLAB + a * 8)
                 out[pl.ds(n * BLOCK + a * 32 + e, 8, stride=4), :] = back[at, :] + moved[at, :]
-
-    @pl.loop(0, NODES)
-    def _(n):
         for q in range(3):
-            forward(n, q).wait_send()
             backward(n, q).wait_send()
 
     for side in range(2):

time: 37.6 us -> 37.4 us (level)
  no operation moved by 1% of the time
where the time goes in v7:
time: 37.4 us; the launch traced here: 37.1 us
  Pallas kernels  36.1 us (97%)
  local copies, waits for them, and re-layouts  1.06 us (3%)
    pallas_call x1, Pallas kernels, local(): pl.pallas_call(body, out_shape=jax.ShapeDtypeStruct((NODES * BLOCK, 128),...  36.1 us
    unnamed x1, local copies, waits for them, and re-layouts  1.06 us

profile of v7, /device:TPU:1, one launch (start us, length us, event | category | flops | bytes accessed | tf_op | source)
XLA Modules:
  0.0 37.1 jit_solution(7257497157331032150)
XLA Ops:
  0.0 36.1 %rate.1 = f32[2560,128]{1,0:T(8,128)S(1)} custom-call(f32[2560,128]{1,0:T(8,128)} %bitcast.25, f32[256,128]{1,0:T(8,128)} %bitcast.26, f32[32,1024]{1,0:T(8,128)} %refs_2_.1, f32[64,128]{1,0:T(8,128)} %bitcast.28, f32[64,128]{1,0:T(8,128)} %bitcast.29, f32[256,128]{1,0:T(8,128)} %bitcast.27, bf16[272,768]{1,0:T(8,128)(2,1)} %constant.12.clone.refs_6_, ...), custom_call_target="tpu_custom_call" | custom-call | tf_op jit(solution)/shard_map/rate/pallas_call | solution.py:732
  36.1 1.1 %copy.23 = f32[4,10,8192]{2,0,1:T(4,128)} copy(f32[4,10,8192]{2,0,1:T(4,128)S(1)} %bitcast.24) | data formatting | bytes 2621440

commit v8 on v7

--- a/solution.py
+++ b/solution.py
@@ -22,7 +22,7 @@
 HALO = TABLE + 5 * 8
 POOL = HALO + 2 * NODES * 8
 LINE = 4
-DIRECT = (24, 24)
+DIRECT = (28, 24)
 
 
 def split(x):
@@ -503,7 +503,7 @@
 
     @pl.loop(0, NODES)
     def _(n):
-        @pl.when(n == 3)
+        @pl.when(n == 1)
         def _():
             send_halos()
 

time: 37.4 us -> 37.6 us (level)
  no operation moved by 1% of the time
where the time goes in v8:
time: 37.6 us; the launch traced here: 37.5 us
  Pallas kernels  36.4 us (97%)
  local copies, waits for them, and re-layouts  1.06 us (3%)
    pallas_call x1, Pallas kernels, local(): pl.pallas_call(body, out_shape=jax.ShapeDtypeStruct((NODES * BLOCK, 128),...  36.4 us
    unnamed x1, local copies, waits for them, and re-layouts  1.06 us

profile of v8, /device:TPU:1, one launch (start us, length us, event | category | flops | bytes accessed | tf_op | source)
XLA Modules:
  0.0 37.5 jit_solution(9426237827719500146)
XLA Ops:
  0.0 36.4 %rate.1 = f32[2560,128]{1,0:T(8,128)S(1)} custom-call(f32[2560,128]{1,0:T(8,128)} %bitcast.25, f32[256,128]{1,0:T(8,128)} %bitcast.26, f32[32,1024]{1,0:T(8,128)} %refs_2_.1, f32[64,128]{1,0:T(8,128)} %bitcast.28, f32[64,128]{1,0:T(8,128)} %bitcast.29, f32[256,128]{1,0:T(8,128)} %bitcast.27, bf16[272,768]{1,0:T(8,128)(2,1)} %constant.12.clone.refs_6_, ...), custom_call_target="tpu_custom_call" | custom-call | tf_op jit(solution)/shard_map/rate/pallas_call | solution.py:732
  36.4 1.1 %copy.23 = f32[4,10,8192]{2,0,1:T(4,128)} copy(f32[4,10,8192]{2,0,1:T(4,128)S(1)} %bitcast.24) | data formatting | bytes 2621440
